TPU v7x, 768 devices: a whole 4x8x12 slice. The times are simulated.
768 devices in a mesh: segment: 2 (over core), expert: 48 (over y_hi, z), dp: 8 (over x, y_lo).
Axes of the slice: x: 4, y: 8 (y_hi: 4, y_lo: 2; y = y_hi * 2 + y_lo), z: 12, core: 2. Of those that a mesh axis runs over, the one named last changes fastest.
Arguments:
- moe_input: bfloat16 [2, 6144, 2688], P('segment', 'expert', 'dp'), may hold values from -64 to 64
- norm_gain: float32 [2688], replicated, may hold values from 0.1 to 1.9
- routes: int32 [2, 6144, 6], P('segment', 'expert'), may hold values from 0 to 95, all different within a row; in each aligned block of 128 rows (0 to 127, 128 to 255, ..., all dimensions but the last counted through in order) at most 9 rows name the same one
- route_scores: float32 [2, 6144, 6], P('segment', 'expert'), may hold values from -8 to 8
- w_up: bfloat16 [96, 2688, 1856], P('expert', None, 'dp'), may hold values from -0.125 to 0.125
- w_down: bfloat16 [96, 1856, 2688], P('expert', None, 'dp'), may hold values from -0.125 to 0.125
- queries: bfloat16 [2, 6144, 2048], P('segment', 'expert', 'dp'), may hold values from -100 to 100
- keys: bfloat16 [2, 6144, 256], P('segment', 'expert'), may hold values from -6 to 6
- values: bfloat16 [2, 6144, 256], P('segment', 'expert'), may hold values from -6 to 6
- out_grad: bfloat16 [2, 6144, 2688], P('segment', 'expert'), may hold values from -6 to 6
- w_query: bfloat16 [2688, 2048], P(None, 'dp'), may hold values from -0.125 to 0.125
- w_key: bfloat16 [2688, 256], replicated, may hold values from -0.125 to 0.125
- w_value: bfloat16 [2688, 256], replicated, may hold values from -0.125 to 0.125
- w_out: bfloat16 [2048, 2688], P('dp'), may hold values from -0.125 to 0.125
Outputs:
- moe_next: bfloat16 [2, 6144, 2688], P('segment', 'expert', 'dp')
- grad_prev: bfloat16 [2, 6144, 2688], P('segment', 'expert', 'dp')
Inputs may be any that keep to these rules, and one draw needn't show every extreme that they name: `routes`: each row names 6 different experts. Among the 128 rows of one sequence no expert is named more than 9 times, a bound that some block reaches; every expert is named by some row.
All inputs are finite; a program needn't handle non-finite values.
Results may differ from a plain program's by a relative error of at most 0.028.
Values may be sent and summed in bfloat16 or wider, within the bound.
A program may use at most 128 MiB of HBM per device.

v0:
```python
import jax
import jax.numpy as jnp
from jax import lax
from jax.sharding import Mesh
from jax.sharding import PartitionSpec as P

D = 2688
HEADS = 16
KV_HEADS = 2
HEAD_DIM = 128
TOPK = 6
DP = ("dp_0", "dp_1")


NORM_EPSILON = 1e-05


def gather_axes(array, axes, dim):
    if not axes:
        return array
    nearer = lax.all_gather(array, axes[-1], axis=dim, tiled=True)
    return gather_axes(nearer, axes[:-1], dim)


def partner(block, axis, distance):
    count = lax.axis_size(axis)
    route = []
    for low in range(count):
        high = low | 1 << distance
        if high != low and high < count:
            route += [(low, high), (high, low)]
    return lax.ppermute(block, axis, route)


def attention_grad(queries, keys, values, out_grad, w_query, w_key, w_value, w_out, block_index):
    token_count = queries.shape[0]
    query_width = queries.shape[1]
    heads_here = query_width // HEAD_DIM
    group_size = HEADS // KV_HEADS
    score_scale = HEAD_DIM ** (-0.5)
    head_group = block_index * heads_here // group_size
    kv_start = head_group * HEAD_DIM
    key_head = lax.dynamic_slice_in_dim(keys, kv_start, HEAD_DIM, 1)
    value_head = lax.dynamic_slice_in_dim(values, kv_start, HEAD_DIM, 1)
    key_weight = lax.dynamic_slice_in_dim(w_key, kv_start, HEAD_DIM, 1)
    value_weight = lax.dynamic_slice_in_dim(w_value, kv_start, HEAD_DIM, 1)
    d_attn = jnp.einsum("td,qd->tq", out_grad, w_out, preferred_element_type=jnp.float32).astype(
        jnp.bfloat16
    )
    grad_heads = d_attn.reshape(token_count, heads_here, HEAD_DIM)
    query_heads = queries.reshape(token_count, heads_here, HEAD_DIM)
    scores = (
        jnp.einsum("ihd,jd->hij", query_heads, key_head, preferred_element_type=jnp.float32)
        * score_scale
    )
    positions = jnp.arange(token_count, dtype=jnp.int32)
    causal = positions[None, :] <= positions[:, None]
    scores = jnp.where(causal[None], scores, -jnp.inf)
    peak = jnp.max(scores, axis=2, keepdims=True)
    raised = jnp.exp(scores - peak)
    attn_weights = raised / jnp.sum(raised, axis=2, keepdims=True)
    d_weights = jnp.einsum(
        "ihd,jd->hij", grad_heads, value_head, preferred_element_type=jnp.float32
    )
    row_delta = jnp.sum(attn_weights * d_weights, axis=2, keepdims=True)
    d_scores = (attn_weights * (d_weights - row_delta)).astype(jnp.bfloat16)
    d_query = (
        jnp.einsum("hij,jd->ihd", d_scores, key_head, preferred_element_type=jnp.float32)
        * score_scale
    )
    d_query = d_query.astype(jnp.bfloat16).reshape(token_count, query_width)
    d_key = (
        jnp.einsum("hij,ihd->jd", d_scores, query_heads, preferred_element_type=jnp.float32)
        * score_scale
    ).astype(jnp.bfloat16)
    d_value = jnp.einsum(
        "hij,ihd->jd",
        attn_weights.astype(jnp.bfloat16),
        grad_heads,
        preferred_element_type=jnp.float32,
    ).astype(jnp.bfloat16)
    grad_term = jnp.einsum("tq,dq->td", d_query, w_query, preferred_element_type=jnp.float32)
    grad_term = grad_term + jnp.einsum(
        "tk,dk->td", d_key, key_weight, preferred_element_type=jnp.float32
    )
    grad_term = grad_term + jnp.einsum(
        "tk,dk->td", d_value, value_weight, preferred_element_type=jnp.float32
    )
    return grad_term


def block_product(block_rows, w_up, first_feature):
    width = block_rows.shape[3]
    weight_rows = lax.dynamic_slice_in_dim(w_up, first_feature, width, 1)
    product = jnp.einsum(
        "sjcw,jwh->sjch", block_rows, weight_rows, preferred_element_type=jnp.float32
    )
    return lax.optimization_barrier(product.astype(jnp.bfloat16)).astype(jnp.float32)


def on_device(
    moe_input,
    norm_gain,
    routes,
    route_scores,
    w_up,
    w_down,
    queries,
    keys,
    values,
    out_grad,
    w_query,
    w_key,
    w_value,
    w_out,
):
    columns = lax.axis_size("expert")
    token_count = moe_input.shape[1]
    feature_share = moe_input.shape[2]
    local_experts = w_up.shape[0]
    hidden_share = w_up.shape[2]
    expert_count = local_experts * columns
    capacity = (9 * token_count * TOPK + 8 * expert_count - 1) // (8 * expert_count)
    slot_count = expert_count * capacity
    feature_index = lax.axis_index(DP)
    token_rows = moe_input[0]
    chosen_experts = routes[0]
    logits = route_scores[0]
    flat_choices = chosen_experts.reshape(-1)
    expert_hits = (
        flat_choices[:, None] == jnp.arange(expert_count, dtype=jnp.int32)[None, :]
    ).astype(jnp.int32)
    earlier = jnp.cumsum(expert_hits, axis=0) - expert_hits
    places = jnp.sum(earlier * expert_hits, axis=1).reshape(token_count, TOPK)
    targets = chosen_experts * capacity + places
    slot_ids = jnp.arange(slot_count, dtype=jnp.int32)
    signal = jax.nn.sigmoid(logits)
    gate_values = (
        (signal / jnp.sum(signal, axis=1, keepdims=True)).astype(jnp.bfloat16).astype(jnp.float32)
    )
    spread_sum = jnp.zeros((token_count, slot_count), jnp.float32)
    mixing_sum = jnp.zeros((token_count, slot_count), jnp.float32)
    for choice_index in range(TOPK):
        hit = slot_ids[None, :] == targets[:, choice_index : choice_index + 1]
        spread_sum = spread_sum + hit.astype(jnp.float32)
        mixing_sum = mixing_sum + jnp.where(
            hit, gate_values[:, choice_index : choice_index + 1], 0.0
        )
    spread = spread_sum.astype(jnp.bfloat16)
    mixing = mixing_sum.astype(jnp.bfloat16)
    outgoing = jnp.einsum(
        "ts,tw->sw", spread, token_rows, preferred_element_type=jnp.float32
    ).astype(jnp.bfloat16)
    outgoing = outgoing.reshape(columns, local_experts, capacity, feature_share)
    arrived = lax.all_to_all(outgoing, "expert", split_axis=0, concat_axis=0, tiled=True)
    start_up = jnp.zeros((columns, local_experts, capacity, hidden_share), jnp.float32)
    start_squares = jnp.zeros((columns, local_experts, capacity), jnp.float32)
    piece = gather_axes(arrived, DP, 3)
    start = jnp.int32(0)
    running = start_up
    squares_run = start_squares
    for block_number in range(piece.shape[3] // feature_share):
        first = block_number * feature_share
        block_rows = piece[:, :, :, first : first + feature_share].astype(jnp.float32)
        squares_run = squares_run + jnp.sum(jnp.square(block_rows), axis=3)
        gain_block = lax.dynamic_slice_in_dim(norm_gain, first, feature_share, 0)
        scaled_block = (block_rows * gain_block).astype(jnp.bfloat16)
        running = running + block_product(scaled_block, w_up, start + first)
    inverse = 1.0 / jnp.sqrt(squares_run / D + NORM_EPSILON)
    projected = running * inverse[..., None]
    hidden = jnp.square(jnp.maximum(projected, 0.0)).astype(jnp.bfloat16)
    grad_term = attention_grad(
        queries[0], keys[0], values[0], out_grad[0], w_query, w_key, w_value, w_out, feature_index
    )
    grad_here = lax.psum_scatter(
        grad_term.astype(jnp.bfloat16), DP, scatter_dimension=1, tiled=True
    )
    expert_out = jnp.einsum(
        "sjch,jhd->sjcd", gather_axes(hidden, DP, 3), w_down, preferred_element_type=jnp.float32
    )
    expert_rows = expert_out.astype(jnp.bfloat16)
    returned = lax.all_to_all(expert_rows, "expert", split_axis=0, concat_axis=0, tiled=True)
    moe_out = jnp.dot(
        mixing, returned.reshape(slot_count, feature_share), preferred_element_type=jnp.float32
    ).astype(jnp.bfloat16)
    moe_next, grad_prev = partner((moe_out, grad_here), "segment", 0)
    return (moe_next[None], grad_prev[None])


def solution(mesh):
    finer = Mesh(
        mesh.devices.reshape(mesh.shape["segment"], mesh.shape["expert"], 4, 2),
        ("segment", "expert", "dp_0", "dp_1"),
    )
    return jax.shard_map(
        on_device,
        mesh=finer,
        in_specs=(
            P("segment", "expert", DP),
            P(),
            P("segment", "expert", None),
            P("segment", "expert", None),
            P("expert", None, DP),
            P("expert", None, DP),
            P("segment", "expert", DP),
            P("segment", "expert", None),
            P("segment", "expert", None),
            P("segment", "expert", None),
            P(None, DP),
            P(),
            P(),
            P(DP, None),
        ),
        out_specs=(P("segment", "expert", DP), P("segment", "expert", DP)),
        check_vma=False,
    )
```

profile of v0, /device:TPU:6, one launch (start us, length us, event | category | flops | bytes accessed | tf_op | source)
XLA Modules:
  0.0 542.1 jit_solution(4441945817754045250)
XLA Ops:
  9.3 1.9 reduce-window.6
  16.9 1.8 copy.146
  18.7 52.4 %all_to_all.10 = bf16[48,2,9,336]{3,1,2,0:T(2,128)(2,1)S(1)} all-to-all(bf16[48,2,9,336]{3,1,2,0:T(2,128)(2,1)S(1)} %copy.146), channel_id=1, replica_groups=mesh['segment'=2,'expert'=48,'dp_0'=4,'dp_1'=2] {'expert'}, dimensions={0} | all-to-all | bytes 1161216 | tf_op jit(solution)/shard_map/all_to_all | solution.py:155
  71.1 4.4 copy.147
  75.6 47.0 %all-gather.4.cloned.1.call-done = bf16[48,2,9,672]{0,1,2,3:T(2,128)(2,1)} async-done(((bf16[48,2,9,336]{0,1,2,3:T(2,128)(2,1)}), bf16[48,2,9,672]{0,1,2,3:T(2,128)(2,1)}) %all-gather.4.cloned.1.call-update) | async-done | bytes 1161232 | tf_op jit(solution)/shard_map/all_gather | solution.py:21
  124.0 125.3 %all-gather.6.cloned.1.call-done = bf16[48,2,9,2688]{0,1,2,3:T(2,128)(2,1)} async-done(((bf16[48,2,9,672]{0,1,2,3:T(2,128)(2,1)}), bf16[48,2,9,2688]{0,1,2,3:T(2,128)(2,1)}) %all-gather.6.cloned.1.call-update) | async-done | bytes 4644880 | tf_op jit(solution)/shard_map/all_gather | solution.py:21
  249.4 13.4 %fusion.152 = (bf16[48,2,9,336]{0,1,2,3:T(2,128)(2,1)}, bf16[48,2,9,336]{0,1,2,3:T(2,128)(2,1)}, bf16[48,2,9,336]{0,1,2,3:T(2,128)(2,1)}, bf16[48,2,9,336]{0,1,2...) fusion(bf16[48,2,9,2688]{0,1,2,3:T(2,128)(2,1)} %all-gather.6.c, ...), kind=kLoop, calls=%fused_computation.191 | loop fusion | bytes 9289728 | tf_op jit(solution)/shard_map/slice | solution.py:164
  262.7 3.6 copy.204
  266.7 4.2 copy.206
  272.4 4.3 copy.208
  278.0 4.2 copy.210
  283.7 4.2 copy.212
  289.3 4.3 copy.214
  295.0 4.3 copy.216
  301.3 4.2 copy.218
  307.5 1.5 add_rsqrt_fusion
  310.0 1.5 fusion.32
  311.6 1.7 fusion.33
  313.3 1.6 fusion.34
  318.2 2.0 copy.173
  320.2 35.5 %all_gather.14 = bf16[48,2,9,464]{0,1,2,3:T(2,128)(2,1)} all-gather(bf16[48,2,9,232]{0,1,2,3:T(2,128)(2,1)} %copy.173), channel_id=1, replica_groups=mesh['segment'=2,'expert'=48,'dp_0'=4,'dp_1'=2] {'dp_1'}, dimensions={3}, use_global_device_ids=true | all-gather | bytes 1202688 | tf_op jit(solution)/shard_map/all_gather | solution.py:21
  356.8 1.9 fusion.45
  360.2 2.7 fusion.50
  362.9 2.7 fusion.49
  365.6 82.8 %all-gather.8.cloned.1.call-done = bf16[48,2,9,1856]{0,1,2,3:T(2,128)(2,1)} async-done(((bf16[48,2,9,464]{0,1,2,3:T(2,128)(2,1)}), bf16[48,2,9,1856]{0,1,2,3:T(2,128)(2,1)}) %all-gather.8.cloned.1.call-update) | async-done | bytes 3207184 | tf_op jit(solution)/shard_map/all_gather | solution.py:21
  448.4 8.0 %fusion.27 = bf16[48,2,9,336]{3,0,2,1:T(8,128)(2,1)S(1)} fusion(bf16[2,1856,336]{1,2,0:T(8,128)(2,1)S(1)} %copy-done, bf16[48,2,9,1856]{0,1,2,3:T(2,128)(2,1)} %all-gather.8.cloned.1.call-done), kind=kOutput, calls=%fused_computation.41 | convolution fusion | flops 1077898752 | bytes 6282240 | tf_op jit(solution)/shard_map/sjch,jhd->sjcd/dot_general | solution.py:178
  457.8 16.0 %all-to-all-start.1 = ((bf16[48,2,9,336]{3,1,2,0:T(2,128)(2,1)}), bf16[48,2,9,336]{3,1,2,0:T(2,128)(2,1)S(1)}, u32[]{:S(2)}, u32[]{:S(2)}) async-start(bf16[48,2,9,336]{3,1,2,0:T(2,128)(2,1)} %copy.175), calls=%async_computation.1 | async-start | bytes 1327104 | tf_op jit(solution)/shard_map/all_to_all | solution.py:182
  473.8 3.5 fusion.4
  477.5 47.3 %reduce-scatter.2.cloned.1.call-done = bf16[128,336]{0,1:T(8,128)(2,1)} async-done(((bf16[128,2688]{0,1:T(8,128)(2,1)}), bf16[128,336]{0,1:T(8,128)(2,1)}) %reduce-scatter.2.cloned.1.call-update) | async-done | bytes 86032 | tf_op jit(solution)/shard_map/reduce_scatter | solution.py:175
  524.8 1.9 collective-permute-start.1
  527.9 1.6 reshape.97
  530.4 2.4 collective-permute-start
  (131 shorter events, 32.0 us)
Async XLA Ops:
  8.0 440.4 %copy-start = (bf16[2,1856,336]{1,2,0:T(8,128)(2,1)S(1)}, bf16[2,1856,336]{1,2,0:T(8,128)(2,1)}, u32[]{:S(2)}) copy-start(bf16[2,1856,336]{1,2,0:T(8,128)(2,1)} %param.19) | copy-start | bytes 7483396
  8.0 4.8 copy-start.33
  8.0 114.6 %all-gather.4.cloned.1.call-start = ((), (), s32[]{:S(2)}) async-start(), calls=%async_computation.3 | async-start | bytes 4644864 | tf_op jit(solution)/shard_map/all_gather | solution.py:21
  75.6 173.8 %all-gather.6.cloned.1.call-start = ((), (), s32[]{:S(2)}) async-start(), calls=%async_computation.4 | async-start | bytes 15482880 | tf_op jit(solution)/shard_map/all_gather | solution.py:21
  122.7 325.7 %all-gather.8.cloned.1.call-start = ((), (), s32[]{:S(2)}) async-start(), calls=%async_computation.5 | async-start | bytes 10690560 | tf_op jit(solution)/shard_map/all_gather | solution.py:21
  307.5 4.0 copy-start.19
  310.0 1.5 copy-start.1
  310.0 3.3 copy-start.2
  310.0 3.3 copy-start.18
  311.5 3.4 copy-start.3
  311.5 3.4 copy-start.17
  311.5 3.4 copy-start.32
  313.3 2.2 copy-start.4
  313.3 2.2 copy-start.16
  314.9 1.1 copy-start.5
  315.5 1.1 copy-start.6
  315.5 1.1 copy-start.14
  316.0 1.1 copy-start.7
  316.0 1.1 copy-start.13
  355.7 1.1 copy-start.8
  355.7 3.0 copy-start.11
  457.8 68.9 %all-to-all-start.1 = ((bf16[48,2,9,336]{3,1,2,0:T(2,128)(2,1)}), bf16[48,2,9,336]{3,1,2,0:T(2,128)(2,1)S(1)}, u32[]{:S(2)}, u32[]{:S(2)}) async-start(bf16[48,2,9,336]{3,1,2,0:T(2,128)(2,1)} %copy.175), calls=%async_computation.1 | async-start | bytes 1327104 | tf_op jit(solution)/shard_map/all_to_all | solution.py:182
  473.8 51.0 %reduce-scatter.2.cloned.1.call-start = ((), (), s32[]{:S(2)}) async-start(), calls=%async_computation.6 | async-start | bytes 774144 | tf_op jit(solution)/shard_map/reduce_scatter | solution.py:175
  473.8 3.6 copy-start.12
  524.8 8.0 %collective-permute-start.1 = (bf16[128,336]{0,1:T(8,128)(2,1)}, bf16[128,336]{0,1:T(8,128)(2,1)S(1)}, u32[]{:S(2)}, u32[]{:S(2)}) collective-permute-start(bf16[128,336]{0,1:T(8,128)(2,1)} %reduce-scatter.2.cloned.1.call-done), channel_id=1, source_target_pairs={{0,384},{384,0},{1,385},{385,1},{2,386},{386,2},{3,387},{387,3},{4... | collective-permute-start | bytes 258056 | tf_op jit(solution)/shard_map/ppermute | solution.py:32
  527.9 1.7 copy-start.21
  527.9 1.7 copy-start.23
  527.9 1.7 copy-start.25
  527.9 1.7 copy-start.27
  527.9 1.7 copy-start.29
  527.9 1.7 copy-start.31
  530.4 3.3 collective-permute-start
  (9 other events, 5.8 us)
Sparse Core Ops, SparseCore 0:
  75.7 46.8 all-gather.3
  125.0 124.2 all-gather.5
  355.8 92.4 all-gather.7
Sparse Core Ops, SparseCore 1:
  477.5 47.2 reduce-scatter.1
where the time goes:
time: 548 us; the launch traced here: 542 us
  waiting for transfers between devices  303 us (55%)
  blocking collectives  87.9 us (16%)
  local copies, waits for them, and re-layouts  71 us (13%)
  matrix products  29.8 us (5%)
  starting transfers between devices  20.7 us (4%)
  between operations  15.9 us (3%)
  other arithmetic  13.6 us (2%)
    all_gather x3, waiting for transfers between devices, gather_axes(): nearer = lax.all_gather(array, axes[-1], axis=dim, tiled=True)  255 us
    all_to_all x1, blocking collectives, on_device(): lax.all_to_all(outgoing, 'expert', split_axis=0, concat_axis=0, tiled=True)  52.4 us
    reduce_scatter x1, waiting for transfers between devices, on_device(): lax.psum_scatter(grad_term.astype(jnp.bfloat16), DP, scatter_dimension=1,...  47.3 us
    unnamed x87, local copies, waits for them, and re-layouts  39.9 us
    all_gather x1, blocking collectives, gather_axes(): nearer = lax.all_gather(array, axes[-1], axis=dim, tiled=True)  35.5 us
    all_to_all x1, starting transfers between devices, on_device(): lax.all_to_all(expert_rows, 'expert', split_axis=0, concat_axis=0, tiled=...  16 us
    slice x1, local copies, waits for them, and re-layouts, on_device(): block_rows = piece[:, :, :, first:first + feature_share].astype(jnp.float32)  13.4 us
  transfers between devices with their start and end apart: 7, of which 5 were waited for; matrix products, arithmetic and copies ran while one was open for 3% of the time, Pallas kernels for 0%

commit v1 on v0

v1 whole, which is shorter than its diff:
```python
import functools

import jax
import jax.numpy as jnp
from jax import lax
from jax.experimental import pallas as pl
from jax.experimental.pallas import tpu as pltpu
from jax.sharding import Mesh
from jax.sharding import PartitionSpec as P

MESH = pl.DeviceIdType.MESH
F32 = jnp.float32
BF16 = jnp.bfloat16

D = 2688
HID = 1856
HEAD_DIM = 128
TOPK = 6
TOK = 128
CAP = 9
NZ = 12
NYH = 4
NX = 4
FB = 336
FP = 384
HB = 232
HX = 464
HP = 512
SEQS = (7, 5)
ROWS = (64, 48)
FIRST = (0, 7)
LANE_E, LANE_P, LANE_G, LANE_S = 80, 88, 96, 104


def mm(a, b):
    return lax.dot_general(a, b, (((1,), (0,)), ((), ())), preferred_element_type=F32)


def mm_nt(a, b):
    return lax.dot_general(a, b, (((1,), (1,)), ((), ())), preferred_element_type=F32)


def iota(shape, dim):
    return lax.broadcasted_iota(jnp.int32, shape, dim)


def remote(src, dst, sems, index, device):
    return pltpu.make_async_remote_copy(
        src_ref=src,
        dst_ref=dst,
        send_sem=sems[0].at[index],
        recv_sem=sems[1].at[index],
        device_id=device,
        device_id_type=MESH,
    )


def kernel(
    tok_ref, gain_ref, routes_ref, scores_ref, w_up, w_down, queries, keys, values, out_grad,
    w_query, w_key, w_value, w_out,
    moe_out, grad_out,
    ag, sel_a, sel_b, oa, ob, xa, xb, tg, rtg, wu, wuo, wd, wdo, hid_a, hid_b,
    es_a, es_b, ea, eb, mix_a, mix_b, part, rs, gt, gr,
    q_v, k_v, v_v, og_v, wq_v, wkv_v, wo_v, dq_v,
    load_sem,
    ag_s, ag_r, dp_s, dp_r, tg_s, tg_r, w_s, w_r, xg_s, xg_r, hg_s, hg_r, ret_s, ret_r, rs_s, rs_r,
    gr_s, gr_r,
):
    s = lax.axis_index("segment")
    yh = lax.axis_index("yh")
    z = lax.axis_index("z")
    x = lax.axis_index("x")
    yl = lax.axis_index("yl")
    other = 1 - s
    ylo = 1 - yl
    xr, xl = lax.rem(x + 1, NX), lax.rem(x + 3, NX)
    xo = lax.rem(x + 2, NX)
    zr, zl = lax.rem(z + 1, NZ), lax.rem(z + NZ - 1, NZ)
    here = yh * 2 + yl
    sel, o_buf, x_buf, hid = (sel_a, sel_b), (oa, ob), (xa, xb), (hid_a, hid_b)
    es, e_buf, mix = (es_a, es_b), (ea, eb), (mix_a, mix_b)

    barrier = pltpu.get_barrier_semaphore()
    peers = [(s, yh, zr, x, yl), (s, yh, zl, x, yl), (s, yh, z, xr, yl), (s, yh, z, xl, yl)]
    for step in range(4):
        row = lax.rem(yh + step, NYH)
        for o in range(2):
            col = yl if o == 0 else ylo
            peers.append((other, row, z, x, col))
            if step or o:
                peers.append((s, row, z, x, col))
            if step:
                peers.append((other, yh, z, lax.rem(x + step, NX), col))
    for peer in peers:
        pl.semaphore_signal(barrier, inc=1, device_id=peer, device_id_type=MESH)

    group = pl.multiple_of((x // 2) * HEAD_DIM, HEAD_DIM)
    loads = [
        (out_grad, og_v),
        (w_out, wo_v),
        (queries, q_v),
        (keys.at[:, pl.ds(group, HEAD_DIM)], k_v),
        (values.at[:, pl.ds(group, HEAD_DIM)], v_v),
        (w_query, wq_v),
        (w_key.at[:, pl.ds(group, HEAD_DIM)], wkv_v.at[:, pl.ds(0, HEAD_DIM)]),
        (w_value.at[:, pl.ds(group, HEAD_DIM)], wkv_v.at[:, pl.ds(HEAD_DIM, HEAD_DIM)]),
        (w_up.at[yl], wu),
        (w_down.at[yl], wd),
    ]
    loads = [pltpu.make_async_copy(a, b, load_sem.at[i]) for i, (a, b) in enumerate(loads)]
    for load in loads:
        load.start()

    wide = tok_ref[...].astype(F32)
    squares = jnp.sum(wide * wide, axis=1, keepdims=True)
    square_hi = squares.astype(BF16).astype(F32)
    square_lo = squares - square_hi
    scaled = wide * gain_ref[...]
    lanes = iota((TOK, 128), 1)
    rows = iota((TOK, 128), 0)
    chosen = routes_ref[...]
    signal = 1.0 / (1.0 + jnp.exp(-scores_ref[...]))
    gates = signal / jnp.sum(signal, axis=1, keepdims=True)
    hits = jnp.zeros((TOK, 128), F32)
    for k in range(TOPK):
        hits = hits + jnp.where(chosen[:, k : k + 1] == lanes, 1.0, 0.0)
    earlier = mm(jnp.where(lanes < rows, 1.0, 0.0).astype(BF16), hits.astype(BF16)) + 1.0
    tail = scaled[:, 256:]
    for k in range(TOPK):
        expert = chosen[:, k : k + 1]
        place = jnp.sum(jnp.where(expert == lanes, earlier, 0.0), axis=1, keepdims=True)
        tail = jnp.where(lanes == LANE_E + k, expert.astype(F32), tail)
        tail = jnp.where(lanes == LANE_P + k, place, tail)
        tail = jnp.where(lanes == LANE_G + k, gates[:, k : k + 1], tail)
    tail = jnp.where(lanes == LANE_S, square_hi, tail)
    tail = jnp.where(lanes == LANE_S + 1, square_lo, tail)
    ag[0, :, 0:256] = scaled[:, :256].astype(BF16)
    ag[0, :, 256:384] = tail.astype(BF16)
    sel_a[...] = jnp.zeros_like(sel_a)
    sel_b[...] = jnp.zeros_like(sel_b)
    eb[:, 48:64, :] = jnp.zeros((8, 16, FP), BF16)

    pl.semaphore_wait(barrier, len(peers))

    def right(k):
        return remote(ag.at[max(2 * k - 3, 0)], ag.at[2 * k - 1], (ag_s, ag_r), 2 * k - 1, (s, yh, zr, x, yl))

    def left(k):
        return remote(ag.at[2 * k - 2], ag.at[2 * k], (ag_s, ag_r), 2 * k, (s, yh, zl, x, yl))

    sent = []

    def start(copy):
        copy.start()
        sent.append(copy)
        return copy

    hops = {1: (start(right(1)), start(left(1)))}
    half_up, half_down = D // 2, HID // 2
    up_rows = pl.ds(pl.multiple_of(s * half_up, 16), half_up)
    down_rows = pl.ds(pl.multiple_of(s * half_down, 16), half_down)
    swap_up = start(remote(w_up.at[ylo, up_rows], wuo.at[up_rows], (w_s, w_r), 0, (s, yh, z, x, ylo)))

    column = iota((8, 128), 0)
    my_experts = (lax.shift_right_logical(column, 1) * (2 * NZ) + 2 * z + jnp.bitwise_and(column, 1)).astype(F32)

    def take(slot):
        chunk = 0 if slot < FIRST[1] else 1
        at = slot - FIRST[chunk]
        info = jnp.transpose(ag[slot, :, 256:384].astype(F32))
        place = jnp.zeros((8, 128), F32)
        gate = jnp.zeros((8, 128), F32)
        for k in range(TOPK):
            mine = info[LANE_E + k : LANE_E + k + 1, :] == my_experts
            place = place + jnp.where(mine, info[LANE_P + k : LANE_P + k + 1, :], 0.0)
            gate = gate + jnp.where(mine, info[LANE_G + k : LANE_G + k + 1, :], 0.0)
        tg[slot * 16 : slot * 16 + 16, :] = jnp.concatenate([place, gate], axis=0).astype(BF16)
        target = jnp.where(place > 0.0, place + (at * CAP - 1.0), -1.0).astype(jnp.int32)
        count = ROWS[chunk]
        slots = iota((count, 128), 0)
        for y in range(8):
            block = jnp.where(slots == target[y : y + 1, :], 1.0, 0.0).astype(BF16)
            sel[chunk][y * count : (y + 1) * count, at * TOK : (at + 1) * TOK] = block

    def dispatch(chunk):
        n, count = SEQS[chunk], ROWS[chunk]
        blocks = ag[FIRST[chunk] : FIRST[chunk] + n].reshape(n * TOK, FP)
        picked = mm(sel[chunk][...], blocks).astype(BF16)
        o_buf[chunk][...] = picked.reshape(8, count, FP)
        copies = []
        for step in range(4):
            row = lax.rem(yh + step, NYH)
            for o in range(2):
                col = yl if o == 0 else ylo
                copies.append(
                    start(
                        remote(
                            o_buf[chunk].at[row * 2 + col],
                            x_buf[chunk].at[x, yl, pl.ds(pl.multiple_of(yh * count, 16), count)],
                            (dp_s, dp_r),
                            chunk * 8 + step * 2 + o,
                            (other, row, z, x, col),
                        )
                    )
                )
        return copies

    def attention_in():
        for load in loads[:5]:
            load.wait()
        d_attn = mm_nt(og_v[...], wo_v[...]).astype(BF16)
        key, value = k_v[...], v_v[...]
        scale = HEAD_DIM ** (-0.5)
        causal = lanes <= rows
        d_key = jnp.zeros((TOK, HEAD_DIM), F32)
        d_value = jnp.zeros((TOK, HEAD_DIM), F32)
        for h in range(2):
            span = slice(h * HEAD_DIM, (h + 1) * HEAD_DIM)
            query, grad = q_v[:, span], d_attn[:, span]
            score = jnp.where(causal, mm_nt(query, key) * scale, -jnp.inf)
            raised = jnp.exp(score - jnp.max(score, axis=1, keepdims=True))
            weights = raised / jnp.sum(raised, axis=1, keepdims=True)
            d_weights = mm_nt(grad, value)
            delta = jnp.sum(weights * d_weights, axis=1, keepdims=True)
            d_scores = weights * (d_weights - delta)
            dq_v[:, span] = (mm(d_scores.astype(BF16), key) * scale).astype(BF16)
            d_key = d_key + mm(jnp.transpose(d_scores).astype(BF16), query)
            d_value = d_value + mm(jnp.transpose(weights).astype(BF16), grad)
        dq_v[:, 256:384] = (d_key * scale).astype(BF16)
        dq_v[:, 384:512] = d_value.astype(BF16)

    grads = []

    def attention_out(step):
        if step == 0:
            for load in loads[5:8]:
                load.wait()
        to = lax.rem(x + step, NX)
        for o in range(2):
            col = yl if o == 0 else ylo
            block = pl.ds(pl.multiple_of((to * 2 + col) * FB, 16), FB)
            term = mm_nt(dq_v[:, 0:256], wq_v[block, :]) + mm_nt(dq_v[:, 256:512], wkv_v[block, :])
            gt[step * 2 + o, :, 0:FB] = term.astype(BF16)
            grads.append(
                start(remote(gt.at[step * 2 + o], gr.at[step * 2 + o], (gr_s, gr_r), step * 2 + o, (other, yh, z, to, col)))
            )

    def hop(k):
        hops[k][0].wait_recv()
        later = [start(right(k + 1))] if k < 6 else []
        if k < 6:
            hops[k][1].wait_recv()
            if k < 5:
                later.append(start(left(k + 1)))
        hops[k + 1] = tuple(later)

    take(0)
    hop(1)
    take(1)
    take(2)
    attention_in()
    hop(2)
    take(3)
    take(4)
    attention_out(0)
    hop(3)
    take(5)
    take(6)
    arrive_a = dispatch(0)
    hop(4)
    take(7)
    take(8)
    attention_out(1)
    hop(5)
    take(9)
    take(10)
    hop(6)
    take(11)
    arrive_b = dispatch(1)
    table = start(remote(tg, rtg, (tg_s, tg_r), 0, (other, yh, z, x, yl)))
    swap_up.wait_recv()
    share_up = start(remote(wuo.at[up_rows], wuo.at[up_rows], (w_s, w_r), 1, (other, yh, z, x, yl)))
    attention_out(2)
    attention_out(3)

    def spread(buf, sems, chunk):
        a = start(remote(buf.at[x], buf.at[x], sems, chunk * 4, (s, yh, z, xr, yl)))
        b = start(remote(buf.at[x], buf.at[x], sems, chunk * 4 + 1, (s, yh, z, xl, yl)))
        return a, b

    def relay(buf, sems, chunk, nearer, lower, upper):
        nearer[0].wait_recv()
        a = start(remote(buf.at[(xl, *lower)], buf.at[(xl, *lower)], sems, chunk * 4 + 2, (s, yh, z, xr, yl)))
        nearer[1].wait_recv()
        b = start(remote(buf.at[(xr, *upper)], buf.at[(xr, *upper)], sems, chunk * 4 + 3, (s, yh, z, xl, yl)))
        return a, b

    up_sems, hid_sems = (xg_s, xg_r), (hg_s, hg_r)
    for copy in arrive_a:
        copy.wait_recv()
    near_a = spread(xa, up_sems, 0)
    for copy in arrive_b:
        copy.wait_recv()
    near_b = spread(xb, up_sems, 1)
    swap_down = start(remote(w_down.at[ylo, down_rows], wdo.at[down_rows], (w_s, w_r), 2, (s, yh, z, x, ylo)))
    far_a = relay(xa, up_sems, 0, near_a, (0,), (1,))

    table.wait_recv()

    def mixing(slot, turned, base):
        chunk = 0 if slot < FIRST[1] else 1
        at = slot - FIRST[chunk]
        for pair in range(4):
            c = slot * 16 - base + 2 * pair
            low = lanes < 64
            place = jnp.where(low, turned[:, c : c + 1], turned[:, c + 1 : c + 2])
            gate = jnp.where(low, turned[:, c + 8 : c + 9], turned[:, c + 9 : c + 10])
            slots = jnp.bitwise_and(lanes, 63).astype(F32)
            hit = jnp.logical_and(place > 0.0, slots == place + (at * CAP - 1.0))
            mix[chunk][at * TOK : (at + 1) * TOK, pair * 128 : (pair + 1) * 128] = jnp.where(hit, gate, 0.0).astype(BF16)

    turned = jnp.transpose(rtg[0:128, :].astype(F32))
    for slot in range(8):
        mixing(slot, turned, 0)
    turned = jnp.transpose(rtg[64:192, :].astype(F32))
    for slot in range(8, 12):
        mixing(slot, turned, 64)

    loads[8].wait()
    share_up.wait_recv()

    def place_hidden(which):
        return jnp.where(iota((HB, HP), 1) == iota((HB, HP), 0) + which * HB, 1.0, 0.0).astype(BF16)

    def up(chunk, far):
        buf = x_buf[chunk]
        count = 4 * ROWS[chunk]
        mine = jnp.zeros((count, HB), F32)
        theirs = jnp.zeros((count, HB), F32)
        sums = jnp.zeros((count, 128), F32)
        for index, owner in enumerate((x, xl, xr, xo)):
            for part_of in range(2):
                if index == 3:
                    far[part_of].wait_recv()
                first = pl.ds(pl.multiple_of((owner * 2 + part_of) * FB, 16), FB)
                block = buf[owner, part_of, :, 0:FB]
                mine = mine + mm(block, wu[first, :])
                theirs = theirs + mm(block, wuo[first, :])
                sums = sums + buf[owner, part_of, :, 256:384].astype(F32)
        lane = iota((count, 128), 1)
        kept = jnp.where(jnp.logical_or(lane == LANE_S, lane == LANE_S + 1), sums, 0.0)
        inverse = 1.0 / jnp.sqrt(jnp.sum(kept, axis=1, keepdims=True) / D + 1e-5)
        mine = jnp.square(jnp.maximum(mine * inverse, 0.0)).astype(BF16)
        theirs = jnp.square(jnp.maximum(theirs * inverse, 0.0)).astype(BF16)
        hid[chunk][x] = (mm(mine, place_hidden(yl)) + mm(theirs, place_hidden(ylo))).astype(BF16)
        return spread(hid[chunk], hid_sems, chunk)

    hid_near_a = up(0, far_a)
    far_b = relay(xb, up_sems, 1, near_b, (0,), (1,))
    hid_far_a = relay(hid_a, hid_sems, 0, hid_near_a, (pl.ds(0, 128),), (pl.ds(128, 128),))
    hid_near_b = up(1, far_b)
    hid_far_b = relay(hid_b, hid_sems, 1, hid_near_b, (pl.ds(0, 96),), (pl.ds(96, 96),))
    swap_down.wait_recv()
    share_down = start(remote(wdo.at[down_rows], wdo.at[down_rows], (w_s, w_r), 3, (other, yh, z, x, yl)))
    loads[9].wait()
    share_down.wait_recv()

    def down(chunk, far):
        count = ROWS[chunk]
        buf = hid[chunk]
        mine = jnp.zeros((4 * count, FB), F32)
        theirs = jnp.zeros((4 * count, FB), F32)
        for index, owner in enumerate((x, xl, xr, xo)):
            if index == 3:
                far[0].wait_recv()
                far[1].wait_recv()
            first = pl.ds(pl.multiple_of(owner * HX, 16), HX)
            block = buf[owner, :, 0:HX]
            mine = mine + mm(block, wd[first, :])
            theirs = theirs + mm(block, wdo[first, :])
        es[chunk][0, :, 0:FB] = mine.astype(BF16)
        es[chunk][1, :, 0:FB] = theirs.astype(BF16)
        copies = []
        for step in range(4):
            row = lax.rem(yh + step, NYH)
            span = pl.ds(pl.multiple_of(row * count, 16), count)
            for o in range(2):
                source = es[chunk].at[o, span]
                target = e_buf[chunk].at[here, pl.ds(0, count)]
                index = chunk * 8 + step * 2 + o
                if step or o:
                    copies.append(
                        start(remote(source, target, (ret_s, ret_r), index, (s, row, z, x, yl if o == 0 else ylo)))
                    )
                else:
                    local = pltpu.make_async_copy(source, target, ret_r.at[index])
                    local.start()
                    copies.append(local)
        return copies

    def landed(copies):
        copies[0].wait()
        for copy in copies[1:]:
            copy.wait_recv()

    back_a = down(0, hid_far_a)
    back_b = down(1, hid_far_b)

    def combine(chunk):
        n = SEQS[chunk]
        rows_of = e_buf[chunk][...].reshape(512, FP)
        part[FIRST[chunk] : FIRST[chunk] + n] = mm(mix[chunk][...], rows_of).astype(BF16).reshape(n, TOK, FP)

    landed(back_a)
    combine(0)
    landed(back_b)
    combine(1)

    def sum_right(k):
        return remote(part.at[11 if k == 6 else 2 * k], rs.at[k - 1], (rs_s, rs_r), k - 1, (s, yh, zr, x, yl))

    def sum_left(k):
        return remote(part.at[2 * k - 1], rs.at[5 + k], (rs_s, rs_r), 5 + k, (s, yh, zl, x, yl))

    forward = start(sum_right(6))
    backward = start(sum_left(5))
    total = jnp.zeros((TOK, FP), F32)
    for copy in grads[:1]:
        copy.wait_recv()
    total = gr[0].astype(F32)
    for i in range(1, 8):
        grads[i].wait_recv()
        total = total + gr[i].astype(F32)
    grad_out[0] = total[:, :FB].astype(BF16)
    for k in range(5, 0, -1):
        forward.wait_recv()
        part[2 * k] = (part[2 * k].astype(F32) + rs[k].astype(F32)).astype(BF16)
        forward = start(sum_right(k))
        if k > 1:
            backward.wait_recv()
            at = 2 * (k - 1) - 1
            part[at] = (part[at].astype(F32) + rs[5 + k].astype(F32)).astype(BF16)
            backward = start(sum_left(k - 1))
    forward.wait_recv()
    backward.wait_recv()
    total = part[0].astype(F32) + rs[0].astype(F32) + rs[6].astype(F32)
    moe_out[0] = total[:, :FB].astype(BF16)
    for copy in sent:
        copy.wait_send()


def on_device(
    moe_input, norm_gain, routes, route_scores, w_up, w_down, queries, keys, values, out_grad,
    w_query, w_key, w_value, w_out,
):
    tokens = jnp.pad(moe_input[0], ((0, 0), (0, FP - FB)))
    gain = jnp.pad(norm_gain, (0, FP - FB)).reshape(1, FP)
    anywhere = pl.BlockSpec(memory_space=pl.ANY)
    vmem = pl.BlockSpec(memory_space=pltpu.VMEM)
    dma = pltpu.SemaphoreType.DMA

    def vm(*shape):
        return pltpu.VMEM(shape, BF16)

    scratch = [
        vm(12, TOK, FP),
        vm(512, 896), vm(384, 640),
        vm(8, 64, FP), vm(8, 48, FP),
        vm(4, 2, 256, FP), vm(4, 2, 192, FP),
        vm(192, 128), vm(192, 128),
        vm(D, HB), vm(D, HB),
        vm(HID, FB), vm(HID, FB),
        vm(4, 256, HP), vm(4, 192, HP),
        vm(2, 256, FP), vm(2, 192, FP),
        vm(8, 64, FP), vm(8, 64, FP),
        vm(896, 512), vm(640, 512),
        vm(12, TOK, FP), vm(11, TOK, FP),
        vm(8, TOK, FP), vm(8, TOK, FP),
        vm(TOK, 256), vm(TOK, 128), vm(TOK, 128), vm(TOK, D),
        vm(D, 256), vm(D, 256), vm(256, D), vm(TOK, 512),
        dma((10,)),
        dma((12,)), dma((12,)),
        dma((16,)), dma((16,)),
        dma((1,)), dma((1,)),
        dma((4,)), dma((4,)),
        dma((8,)), dma((8,)),
        dma((8,)), dma((8,)),
        dma((16,)), dma((16,)),
        dma((11,)), dma((11,)),
        dma((8,)), dma((8,)),
    ]
    block = jax.ShapeDtypeStruct((1, TOK, FB), BF16)
    return pl.pallas_call(
        kernel,
        name="sections",
        out_shape=(block, block),
        in_specs=[vmem] * 4 + [anywhere] * 10,
        out_specs=(vmem, vmem),
        scratch_shapes=scratch,
        compiler_params=pltpu.CompilerParams(
            collective_id=0, has_side_effects=True, vmem_limit_bytes=56 * 2**20
        ),
    )(
        tokens, gain, routes[0], route_scores[0], w_up, w_down, queries[0], keys[0], values[0], out_grad[0],
        w_query, w_key, w_value, w_out,
    )


def solution(mesh):
    finer = Mesh(
        mesh.devices.reshape(2, NYH, NZ, NX, 2), ("segment", "yh", "z", "x", "yl")
    )
    expert, dp = ("yh", "z"), ("x", "yl")
    return jax.shard_map(
        on_device,
        mesh=finer,
        in_specs=(
            P("segment", expert, dp),
            P(dp),
            P("segment", expert, None),
            P("segment", expert, None),
            P(expert, None, dp),
            P(expert, None, dp),
            P("segment", expert, dp),
            P("segment", expert, None),
            P("segment", expert, None),
            P("segment", expert, None),
            P(None, dp),
            P(),
            P(),
            P(dp, None),
        ),
        out_specs=(P("segment", expert, dp), P("segment", expert, dp)),
        check_vma=False,
    )
```

time: 548 us -> 158 us (0.29); the launches traced: 542 us -> 158 us
  waiting for transfers between devices: 303 us -> 0 us
  Pallas kernels: 0 us -> 139 us
  blocking collectives: 87.9 us -> 0 us
  local copies, waits for them, and re-layouts: 71 us -> 17.8 us
  matrix products: 29.8 us -> 0 us
  starting transfers between devices: 20.7 us -> 0 us
  between operations: 15.9 us -> 1.3 us
  other arithmetic: 13.6 us -> 0 us
    all_gather x3 -> x0, waiting for transfers between devices: 255 us -> none  [gather_axes(): nearer = lax.all_gather(array, axes[-1], axis=dim, tiled=True)]
    pallas_call x0 -> x1, Pallas kernels: none -> 139 us  [on_device(): pl.pallas_call(kernel, name='sections', out_shape=(block, block), in_spec...]
    all_to_all x1 -> x0, blocking collectives: 52.4 us -> none  [on_device(): lax.all_to_all(outgoing, 'expert', split_axis=0, concat_axis=0, tiled=True)]
    reduce_scatter x1 -> x0, waiting for transfers between devices: 47.3 us -> none  [on_device(): lax.psum_scatter(grad_term.astype(jnp.bfloat16), DP, scatter_dimension=1,...]
    all_gather x1 -> x0, blocking collectives: 35.5 us -> none  [gather_axes(): nearer = lax.all_gather(array, axes[-1], axis=dim, tiled=True)]
    dot_general x17 -> x0, matrix products: 29.6 us -> none  [the longest x1 8.04 us: on_device(): jnp.einsum('sjch,jhd->sjcd', gather_axes(hidden, DP, 3), w_down, preferre...]
    unnamed x87 -> x7, local copies, waits for them, and re-layouts: 39.9 us -> 11.3 us
    all_to_all x1 -> x0, starting transfers between devices: 16 us -> none  [on_device(): lax.all_to_all(expert_rows, 'expert', split_axis=0, concat_axis=0, tiled=...]
  transfers between devices with their start and end apart: 7 -> 0, of which waited for: 5 -> 0; matrix products, arithmetic and copies ran while one was open for 3% -> 0% of each run, Pallas kernels for 0% -> 0%
where the time goes in v1:
time: 158 us
  Pallas kernels  139 us (88%)
  local copies, waits for them, and re-layouts  17.8 us (11%)
    pallas_call x1, Pallas kernels, on_device(): pl.pallas_call(kernel, name='sections', out_shape=(block, block), in_spec...  139 us
    unnamed x7, local copies, waits for them, and re-layouts  11.3 us
    pallas_call x2, local copies, waits for them, and re-layouts, on_device(): pl.pallas_call(kernel, name='sections', out_shape=(block, block), in_spec...  3.26 us

profile of v1, /device:TPU:6, one launch (start us, length us, event | category | flops | bytes accessed | tf_op | source)
XLA Modules:
  0.0 157.7 jit_solution(12572452428275669412)
XLA Ops:
  0.6 1.3 dynamic-slice
  2.6 0.8 dynamic-slice.2
  3.3 0.6 reshape.9.gain_ref
  3.9 1.4 copy.17
  5.3 1.4 copy.18
  6.7 1.0 copy.16
  7.7 0.7 pad.8.tok_ref
  8.4 0.0 copy-start
  8.4 4.6 %copy.19.w_up = bf16[2,2688,232]{2,1,0:T(8,128)(2,1)} copy(bf16[2,2688,232]{1,2,0:T(8,128)(2,1)} %param.18) | data formatting | bytes 4988928 | tf_op args[4]
  13.0 0.0 copy-done
  13.0 2.8 %copy.20.w_down = bf16[2,1856,336]{2,1,0:T(8,128)(2,1)} copy(bf16[2,1856,336]{1,2,0:T(8,128)(2,1)S(1)} %copy-done) | data formatting | bytes 4988928 | tf_op args[5]
  15.8 138.5 %sections.1 = (bf16[1,128,336]{2,1,0:T(8,128)(2,1)}, bf16[1,128,336]{2,1,0:T(8,128)(2,1)}) custom-call(bf16[128,384]{1,0:T(8,128)(2,1)} %pad.8.tok_ref, f32[1,384]{1,0:T(1,128)} %reshape.9.gain_ref, s32[128,6]{1,0:T(8,128)} %bitcast.10, f32[128,6]{1,0:T(8,128)} %bitcast.11, bf16[2,2688,232]{2,1,0:T(8,128)(2,1)} %copy.19.w_up, ...), custom_call_target="tpu_custom_call" | custom-call | tf_op jit(solution)/shard_map/sections/pallas_call | solution.py:493
  154.4 1.6 %copy.21 = bf16[1,128,336]{1,2,0:T(8,128)(2,1)} copy(bf16[1,128,336]{2,1,0:T(8,128)(2,1)} %get-tuple-element.2) | data formatting | bytes 172032 | tf_op jit(solution)/shard_map/sections/pallas_call | solution.py:493
  156.0 1.6 %copy.22 = bf16[1,128,336]{1,2,0:T(8,128)(2,1)} copy(bf16[1,128,336]{2,1,0:T(8,128)(2,1)} %get-tuple-element.3) | data formatting | bytes 172032 | tf_op jit(solution)/shard_map/sections/pallas_call | solution.py:493
  (1 shorter events, 0.0 us)
Async XLA Ops:
  8.4 4.6 %copy-start = (bf16[2,1856,336]{1,2,0:T(8,128)(2,1)S(1)}, bf16[2,1856,336]{1,2,0:T(8,128)(2,1)}, u32[]{:S(2)}) copy-start(bf16[2,1856,336]{1,2,0:T(8,128)(2,1)} %param.19) | copy-start | bytes 7483396

commit v2 on v1

--- a/solution.py
+++ b/solution.py
@@ -1,5 +1,3 @@
-import functools
-
 import jax
 import jax.numpy as jnp
 from jax import lax
@@ -59,7 +57,7 @@
     tok_ref, gain_ref, routes_ref, scores_ref, w_up, w_down, queries, keys, values, out_grad,
     w_query, w_key, w_value, w_out,
     moe_out, grad_out,
-    ag, sel_a, sel_b, oa, ob, xa, xb, tg, rtg, wu, wuo, wd, wdo, hid_a, hid_b,
+    ag, sel_a, sel_b, oa, ob, xa, xb, tg, rtg, wut, wuto, wdt, wdto, wu, wuo, wd, wdo, hid_a, hid_b,
     es_a, es_b, ea, eb, mix_a, mix_b, part, rs, gt, gr,
     q_v, k_v, v_v, og_v, wq_v, wkv_v, wo_v, dq_v,
     load_sem,
@@ -104,49 +102,65 @@
         (w_query, wq_v),
         (w_key.at[:, pl.ds(group, HEAD_DIM)], wkv_v.at[:, pl.ds(0, HEAD_DIM)]),
         (w_value.at[:, pl.ds(group, HEAD_DIM)], wkv_v.at[:, pl.ds(HEAD_DIM, HEAD_DIM)]),
-        (w_up.at[yl], wu),
-        (w_down.at[yl], wd),
+        (w_up.at[yl], wut),
+        (w_down.at[yl], wdt),
     ]
     loads = [pltpu.make_async_copy(a, b, load_sem.at[i]) for i, (a, b) in enumerate(loads)]
     for load in loads:
         load.start()
 
+    lanes = iota((TOK, 128), 1)
+    rows = iota((TOK, 128), 0)
     wide = tok_ref[...].astype(F32)
-    squares = jnp.sum(wide * wide, axis=1, keepdims=True)
+    squares = jnp.sum(wide * wide, axis=0, keepdims=True)
     square_hi = squares.astype(BF16).astype(F32)
     square_lo = squares - square_hi
-    scaled = wide * gain_ref[...]
-    lanes = iota((TOK, 128), 1)
-    rows = iota((TOK, 128), 0)
-    chosen = routes_ref[...]
-    signal = 1.0 / (1.0 + jnp.exp(-scores_ref[...]))
-    gates = signal / jnp.sum(signal, axis=1, keepdims=True)
-    hits = jnp.zeros((TOK, 128), F32)
+    experts = iota((96, TOK), 0)
+    hits = jnp.zeros((96, TOK), F32)
+    signals = []
     for k in range(TOPK):
-        hits = hits + jnp.where(chosen[:, k : k + 1] == lanes, 1.0, 0.0)
-    earlier = mm(jnp.where(lanes < rows, 1.0, 0.0).astype(BF16), hits.astype(BF16)) + 1.0
-    tail = scaled[:, 256:]
+        hits = hits + jnp.where(routes_ref[k] == experts, 1.0, 0.0)
+        signals.append(1.0 / (1.0 + jnp.exp(-scores_ref[k])))
+    signal_sum = sum(signals[1:], signals[0])
+    earlier = mm(hits.astype(BF16), jnp.where(rows < lanes, 1.0, 0.0).astype(BF16)) + 1.0
+    info_row = iota((FP - FB, TOK), 0)
+    info = jnp.where(info_row == LANE_S - LANE_E, square_hi, 0.0)
+    info = jnp.where(info_row == LANE_S - LANE_E + 1, square_lo, info)
     for k in range(TOPK):
-        expert = chosen[:, k : k + 1]
-        place = jnp.sum(jnp.where(expert == lanes, earlier, 0.0), axis=1, keepdims=True)
-        tail = jnp.where(lanes == LANE_E + k, expert.astype(F32), tail)
-        tail = jnp.where(lanes == LANE_P + k, place, tail)
-        tail = jnp.where(lanes == LANE_G + k, gates[:, k : k + 1], tail)
-    tail = jnp.where(lanes == LANE_S, square_hi, tail)
-    tail = jnp.where(lanes == LANE_S + 1, square_lo, tail)
-    ag[0, :, 0:256] = scaled[:, :256].astype(BF16)
-    ag[0, :, 256:384] = tail.astype(BF16)
+        expert = routes_ref[k]
+        place = jnp.sum(jnp.where(expert == experts, earlier, 0.0), axis=0, keepdims=True)
+        info = jnp.where(info_row == k, expert.astype(F32), info)
+        info = jnp.where(info_row == LANE_P - LANE_E + k, place, info)
+        info = jnp.where(info_row == LANE_G - LANE_E + k, signals[k] / signal_sum, info)
+    gain_at = (x * 2 + yl) * FB
+    gain_row, gain_lane = gain_at // 128, lax.rem(gain_at, 128)
+    turn = lax.rem(128 - gain_lane, 128)
+    pieces = [
+        pltpu.roll(jnp.broadcast_to(gain_ref[pl.ds(jnp.minimum(gain_row + i, 20), 1), :], (8, 128)), turn, 1)
+        for i in range(4)
+    ]
+    lane8 = iota((8, 128), 1)
+    for i in range(3):
+        source = wide[128 * i : 128 * (i + 1)] if i < 2 else jnp.concatenate([wide[256:], info], axis=0)
+        gain = jnp.where(lane8 < 128 - gain_lane, pieces[i], pieces[i + 1])
+        if i == 2:
+            gain = jnp.where(lane8 < LANE_E, gain, 1.0)
+        ag[0, :, 128 * i : 128 * (i + 1)] = (jnp.transpose(source) * gain[0:1]).astype(BF16)
     sel_a[...] = jnp.zeros_like(sel_a)
     sel_b[...] = jnp.zeros_like(sel_b)
     eb[:, 48:64, :] = jnp.zeros((8, 16, FP), BF16)
 
     pl.semaphore_wait(barrier, len(peers))
 
-    def right(k):
-        return remote(ag.at[max(2 * k - 3, 0)], ag.at[2 * k - 1], (ag_s, ag_r), 2 * k - 1, (s, yh, zr, x, yl))
-
-    def left(k):
-        return remote(ag.at[2 * k - 2], ag.at[2 * k], (ag_s, ag_r), 2 * k, (s, yh, zl, x, yl))
+    def right(k, half):
+        span = pl.ds(64 * half, 64)
+        source, target = max(2 * k - 3, 0), 2 * k - 1
+        return remote(ag.at[source, span], ag.at[target, span], (ag_s, ag_r), 2 * target + half, (s, yh, zr, x, yl))
+
+    def left(k, half):
+        span = pl.ds(64 * half, 64)
+        source, target = 2 * k - 2, 11 if k == 6 else 2 * k
+        return remote(ag.at[source, span], ag.at[target, span], (ag_s, ag_r), 2 * target + half, (s, yh, zl, x, yl))
 
     sent = []
 
@@ -155,11 +169,22 @@
         sent.append(copy)
         return copy
 
-    hops = {1: (start(right(1)), start(left(1)))}
-    half_up, half_down = D // 2, HID // 2
-    up_rows = pl.ds(pl.multiple_of(s * half_up, 16), half_up)
-    down_rows = pl.ds(pl.multiple_of(s * half_down, 16), half_down)
-    swap_up = start(remote(w_up.at[ylo, up_rows], wuo.at[up_rows], (w_s, w_r), 0, (s, yh, z, x, ylo)))
+    def wait_all(*copies):
+        for copy in copies:
+            copy.wait_recv()
+
+    hops = {}
+    for half in range(2):
+        hops[1, half] = (start(right(1, half)), start(left(1, half)))
+    up_cols = pl.ds(pl.multiple_of(s * 1408, 128), 1280)
+    up_middle = pl.ds(1280, 128)
+    down_rows = pl.ds(pl.multiple_of(s * 176, 16), 160)
+    down_middle = pl.ds(160, 16)
+    partner = (s, yh, z, x, ylo)
+    swap_up = (
+        start(remote(w_up.at[ylo, :, up_cols], wuto.at[:, up_cols], (w_s, w_r), 0, partner)),
+        start(remote(w_up.at[ylo, :, up_middle], wuto.at[:, up_middle], (w_s, w_r), 1, partner)),
+    )
 
     column = iota((8, 128), 0)
     my_experts = (lax.shift_right_logical(column, 1) * (2 * NZ) + 2 * z + jnp.bitwise_and(column, 1)).astype(F32)
@@ -205,29 +230,35 @@
                 )
         return copies
 
-    def attention_in():
-        for load in loads[:5]:
-            load.wait()
-        d_attn = mm_nt(og_v[...], wo_v[...]).astype(BF16)
+    d_kv = [jnp.zeros((TOK, HEAD_DIM), F32), jnp.zeros((TOK, HEAD_DIM), F32)]
+    d_attn = {}
+
+    def attention_grad(h):
+        if h == 0:
+            for load in loads[:2]:
+                load.wait()
+        d_attn[h] = mm_nt(og_v[...], wo_v[h * HEAD_DIM : (h + 1) * HEAD_DIM, :]).astype(BF16)
+
+    def attention_in(h):
+        if h == 0:
+            for load in loads[2:5]:
+                load.wait()
         key, value = k_v[...], v_v[...]
         scale = HEAD_DIM ** (-0.5)
-        causal = lanes <= rows
-        d_key = jnp.zeros((TOK, HEAD_DIM), F32)
-        d_value = jnp.zeros((TOK, HEAD_DIM), F32)
-        for h in range(2):
-            span = slice(h * HEAD_DIM, (h + 1) * HEAD_DIM)
-            query, grad = q_v[:, span], d_attn[:, span]
-            score = jnp.where(causal, mm_nt(query, key) * scale, -jnp.inf)
-            raised = jnp.exp(score - jnp.max(score, axis=1, keepdims=True))
-            weights = raised / jnp.sum(raised, axis=1, keepdims=True)
-            d_weights = mm_nt(grad, value)
-            delta = jnp.sum(weights * d_weights, axis=1, keepdims=True)
-            d_scores = weights * (d_weights - delta)
-            dq_v[:, span] = (mm(d_scores.astype(BF16), key) * scale).astype(BF16)
-            d_key = d_key + mm(jnp.transpose(d_scores).astype(BF16), query)
-            d_value = d_value + mm(jnp.transpose(weights).astype(BF16), grad)
-        dq_v[:, 256:384] = (d_key * scale).astype(BF16)
-        dq_v[:, 384:512] = d_value.astype(BF16)
+        span = slice(h * HEAD_DIM, (h + 1) * HEAD_DIM)
+        query, grad = q_v[:, span], d_attn[h]
+        score = jnp.where(lanes <= rows, mm_nt(query, key) * scale, -jnp.inf)
+        raised = jnp.exp(score - jnp.max(score, axis=1, keepdims=True))
+        weights = raised / jnp.sum(raised, axis=1, keepdims=True)
+        d_weights = mm_nt(grad, value)
+        delta = jnp.sum(weights * d_weights, axis=1, keepdims=True)
+        d_scores = weights * (d_weights - delta)
+        dq_v[:, span] = (mm(d_scores.astype(BF16), key) * scale).astype(BF16)
+        d_kv[0] = d_kv[0] + mm(jnp.transpose(d_scores).astype(BF16), query)
+        d_kv[1] = d_kv[1] + mm(jnp.transpose(weights).astype(BF16), grad)
+        if h == 1:
+            dq_v[:, 256:384] = (d_kv[0] * scale).astype(BF16)
+            dq_v[:, 384:512] = d_kv[1].astype(BF16)
 
     grads = []
 
@@ -245,43 +276,68 @@
                 start(remote(gt.at[step * 2 + o], gr.at[step * 2 + o], (gr_s, gr_r), step * 2 + o, (other, yh, z, to, col)))
             )
 
-    def hop(k):
-        hops[k][0].wait_recv()
-        later = [start(right(k + 1))] if k < 6 else []
-        if k < 6:
-            hops[k][1].wait_recv()
-            if k < 5:
-                later.append(start(left(k + 1)))
-        hops[k + 1] = tuple(later)
+    def hop(k, half):
+        wait_all(*hops[k, half])
+        if k < 5:
+            hops[k + 1, half] = (start(right(k + 1, half)), start(left(k + 1, half)))
+        elif k == 5:
+            hops[6, half] = (start(left(6, 1) if half else right(6, 0)),)
 
     take(0)
-    hop(1)
+    attention_grad(0)
+    hop(1, 0)
+    hop(1, 1)
     take(1)
     take(2)
-    attention_in()
-    hop(2)
+    hop(2, 0)
+    attention_grad(1)
+    hop(2, 1)
     take(3)
     take(4)
-    attention_out(0)
-    hop(3)
+    hop(3, 0)
+    attention_in(0)
+    hop(3, 1)
     take(5)
     take(6)
     arrive_a = dispatch(0)
-    hop(4)
+    hop(4, 0)
+    attention_in(1)
+    hop(4, 1)
     take(7)
     take(8)
-    attention_out(1)
-    hop(5)
+    hop(5, 0)
+    attention_out(0)
+    hop(5, 1)
     take(9)
     take(10)
-    hop(6)
+    attention_out(1)
+    hop(6, 0)
+    hop(6, 1)
     take(11)
     arrive_b = dispatch(1)
     table = start(remote(tg, rtg, (tg_s, tg_r), 0, (other, yh, z, x, yl)))
-    swap_up.wait_recv()
-    share_up = start(remote(wuo.at[up_rows], wuo.at[up_rows], (w_s, w_r), 1, (other, yh, z, x, yl)))
+    wait_all(*swap_up)
+    share_up = start(remote(wuto.at[:, up_cols], wuto.at[:, up_cols], (w_s, w_r), 2, (other, yh, z, x, yl)))
     attention_out(2)
     attention_out(3)
+    unit = jnp.where(lanes == rows, 1.0, 0.0).astype(BF16)
+
+    def turn_up(source, target):
+        def step(i, carry):
+            span = pl.ds(pl.multiple_of(i * 128, 128), 128)
+            target[span, :] = mm_nt(unit, source[:, span]).astype(BF16)
+            return carry
+
+        lax.fori_loop(0, D // 128, step, 0)
+
+    def turn_down(source, target):
+        def step(i, carry):
+            span = pl.ds(pl.multiple_of(i * 128, 128), 128)
+            target[span, :] = mm_nt(unit, source[:, span]).astype(BF16)
+            return carry
+
+        lax.fori_loop(0, HID // 128, step, 0)
+        target[1792:1856, :] = mm_nt(unit[0:64, 0:64], source[:, 1792:1856]).astype(BF16)
 
     def spread(buf, sems, chunk):
         a = start(remote(buf.at[x], buf.at[x], sems, chunk * 4, (s, yh, z, xr, yl)))
@@ -296,13 +352,16 @@
         return a, b
 
     up_sems, hid_sems = (xg_s, xg_r), (hg_s, hg_r)
-    for copy in arrive_a:
-        copy.wait_recv()
+    wait_all(*arrive_a)
     near_a = spread(xa, up_sems, 0)
-    for copy in arrive_b:
-        copy.wait_recv()
+    loads[8].wait()
+    turn_up(wut, wu)
+    wait_all(*arrive_b)
     near_b = spread(xb, up_sems, 1)
-    swap_down = start(remote(w_down.at[ylo, down_rows], wdo.at[down_rows], (w_s, w_r), 2, (s, yh, z, x, ylo)))
+    swap_down = (
+        start(remote(w_down.at[ylo, down_rows], wdto.at[down_rows], (w_s, w_r), 3, partner)),
+        start(remote(w_down.at[ylo, down_middle], wdto.at[down_middle], (w_s, w_r), 4, partner)),
+    )
     far_a = relay(xa, up_sems, 0, near_a, (0,), (1,))
 
     table.wait_recv()
@@ -326,8 +385,9 @@
     for slot in range(8, 12):
         mixing(slot, turned, 64)
 
-    loads[8].wait()
     share_up.wait_recv()
+    turn_up(wuto, wuo)
+    far_b = relay(xb, up_sems, 1, near_b, (0,), (1,))
 
     def place_hidden(which):
         return jnp.where(iota((HB, HP), 1) == iota((HB, HP), 0) + which * HB, 1.0, 0.0).astype(BF16)
@@ -356,14 +416,15 @@
         return spread(hid[chunk], hid_sems, chunk)
 
     hid_near_a = up(0, far_a)
-    far_b = relay(xb, up_sems, 1, near_b, (0,), (1,))
+    hid_near_b = up(1, far_b)
+    wait_all(*swap_down)
+    share_down = start(remote(wdto.at[down_rows], wdto.at[down_rows], (w_s, w_r), 5, (other, yh, z, x, yl)))
     hid_far_a = relay(hid_a, hid_sems, 0, hid_near_a, (pl.ds(0, 128),), (pl.ds(128, 128),))
-    hid_near_b = up(1, far_b)
+    loads[9].wait()
+    turn_down(wdt, wd)
     hid_far_b = relay(hid_b, hid_sems, 1, hid_near_b, (pl.ds(0, 96),), (pl.ds(96, 96),))
-    swap_down.wait_recv()
-    share_down = start(remote(wdo.at[down_rows], wdo.at[down_rows], (w_s, w_r), 3, (other, yh, z, x, yl)))
-    loads[9].wait()
     share_down.wait_recv()
+    turn_down(wdto, wdo)
 
     def down(chunk, far):
         count = ROWS[chunk]
@@ -416,35 +477,45 @@
     landed(back_b)
     combine(1)
 
-    def sum_right(k):
-        return remote(part.at[11 if k == 6 else 2 * k], rs.at[k - 1], (rs_s, rs_r), k - 1, (s, yh, zr, x, yl))
-
-    def sum_left(k):
-        return remote(part.at[2 * k - 1], rs.at[5 + k], (rs_s, rs_r), 5 + k, (s, yh, zl, x, yl))
-
-    forward = start(sum_right(6))
-    backward = start(sum_left(5))
-    total = jnp.zeros((TOK, FP), F32)
-    for copy in grads[:1]:
-        copy.wait_recv()
+    def sum_right(k, half):
+        span = pl.ds(64 * half, 64)
+        source = part.at[11 if k == 6 else 2 * k, span]
+        return remote(source, rs.at[k - 1, span], (rs_s, rs_r), 2 * (k - 1) + half, (s, yh, zr, x, yl))
+
+    def sum_left(k, half):
+        span = pl.ds(64 * half, 64)
+        source = part.at[11 if k == 6 else 2 * k - 1, span]
+        return remote(source, rs.at[5 + k, span], (rs_s, rs_r), 2 * (5 + k) + half, (s, yh, zl, x, yl))
+
+    def add(slot, arrived, half):
+        span = slice(64 * half, 64 * half + 64)
+        part[slot, span] = (part[slot, span].astype(F32) + rs[arrived, span].astype(F32)).astype(BF16)
+
+    forward = {0: start(sum_right(6, 0)), 1: start(sum_right(5, 1))}
+    backward = {1: start(sum_left(6, 1)), 0: start(sum_left(5, 0))}
+
+    def write(out, total):
+        for i in range(3):
+            column_block = jnp.transpose(total[:, 128 * i : 128 * (i + 1)]).astype(BF16)
+            out[128 * i : min(128 * (i + 1), FB), :] = column_block if i < 2 else column_block[0 : FB - 256]
+
+    wait_all(*grads)
     total = gr[0].astype(F32)
     for i in range(1, 8):
-        grads[i].wait_recv()
         total = total + gr[i].astype(F32)
-    grad_out[0] = total[:, :FB].astype(BF16)
+    write(grad_out, total)
     for k in range(5, 0, -1):
-        forward.wait_recv()
-        part[2 * k] = (part[2 * k].astype(F32) + rs[k].astype(F32)).astype(BF16)
-        forward = start(sum_right(k))
-        if k > 1:
-            backward.wait_recv()
-            at = 2 * (k - 1) - 1
-            part[at] = (part[at].astype(F32) + rs[5 + k].astype(F32)).astype(BF16)
-            backward = start(sum_left(k - 1))
-    forward.wait_recv()
-    backward.wait_recv()
-    total = part[0].astype(F32) + rs[0].astype(F32) + rs[6].astype(F32)
-    moe_out[0] = total[:, :FB].astype(BF16)
+        for half in range(2):
+            if k < 5 or half == 0:
+                forward[half].wait_recv()
+                add(2 * k, k, half)
+                forward[half] = start(sum_right(k, half))
+            if k < 5 or half == 1:
+                backward[half].wait_recv()
+                add(2 * k - 1, 6 + k, half)
+                backward[half] = start(sum_left(k, half))
+    wait_all(forward[0], backward[0], forward[1], backward[1])
+    write(moe_out, part[0].astype(F32) + rs[0].astype(F32) + rs[6].astype(F32))
     for copy in sent:
         copy.wait_send()
 
@@ -453,8 +524,10 @@
     moe_input, norm_gain, routes, route_scores, w_up, w_down, queries, keys, values, out_grad,
     w_query, w_key, w_value, w_out,
 ):
-    tokens = jnp.pad(moe_input[0], ((0, 0), (0, FP - FB)))
-    gain = jnp.pad(norm_gain, (0, FP - FB)).reshape(1, FP)
+    tokens = jnp.transpose(moe_input[0])
+    gain = norm_gain.reshape(D // 128, 128)
+    routes, route_scores = jnp.transpose(routes, (2, 0, 1)), jnp.transpose(route_scores, (2, 0, 1))
+    w_up, w_down = jnp.transpose(w_up, (0, 2, 1)), jnp.transpose(w_down, (0, 2, 1))
     anywhere = pl.BlockSpec(memory_space=pl.ANY)
     vmem = pl.BlockSpec(memory_space=pltpu.VMEM)
     dma = pltpu.SemaphoreType.DMA
@@ -468,29 +541,30 @@
         vm(8, 64, FP), vm(8, 48, FP),
         vm(4, 2, 256, FP), vm(4, 2, 192, FP),
         vm(192, 128), vm(192, 128),
+        vm(HB, D), vm(HB, D), vm(FB, HID), vm(FB, HID),
         vm(D, HB), vm(D, HB),
         vm(HID, FB), vm(HID, FB),
         vm(4, 256, HP), vm(4, 192, HP),
         vm(2, 256, FP), vm(2, 192, FP),
         vm(8, 64, FP), vm(8, 64, FP),
         vm(896, 512), vm(640, 512),
-        vm(12, TOK, FP), vm(11, TOK, FP),
+        vm(12, TOK, FP), vm(12, TOK, FP),
         vm(8, TOK, FP), vm(8, TOK, FP),
         vm(TOK, 256), vm(TOK, 128), vm(TOK, 128), vm(TOK, D),
         vm(D, 256), vm(D, 256), vm(256, D), vm(TOK, 512),
         dma((10,)),
-        dma((12,)), dma((12,)),
+        dma((24,)), dma((24,)),
         dma((16,)), dma((16,)),
         dma((1,)), dma((1,)),
-        dma((4,)), dma((4,)),
+        dma((6,)), dma((6,)),
         dma((8,)), dma((8,)),
         dma((8,)), dma((8,)),
         dma((16,)), dma((16,)),
-        dma((11,)), dma((11,)),
+        dma((24,)), dma((24,)),
         dma((8,)), dma((8,)),
     ]
-    block = jax.ShapeDtypeStruct((1, TOK, FB), BF16)
-    return pl.pallas_call(
+    block = jax.ShapeDtypeStruct((FB, TOK), BF16)
+    moe_next, grad_prev = pl.pallas_call(
         kernel,
         name="sections",
         out_shape=(block, block),
@@ -501,9 +575,10 @@
             collective_id=0, has_side_effects=True, vmem_limit_bytes=56 * 2**20
         ),
     )(
-        tokens, gain, routes[0], route_scores[0], w_up, w_down, queries[0], keys[0], values[0], out_grad[0],
+        tokens, gain, routes, route_scores, w_up, w_down, queries[0], keys[0], values[0], out_grad[0],
         w_query, w_key, w_value, w_out,
     )
+    return jnp.transpose(moe_next)[None], jnp.transpose(grad_prev)[None]
 
 
 def solution(mesh):
@@ -516,7 +591,7 @@
         mesh=finer,
         in_specs=(
             P("segment", expert, dp),
-            P(dp),
+            P(),
             P("segment", expert, None),
             P("segment", expert, None),
             P(expert, None, dp),

time: 158 us -> 135 us (0.85)
  local copies, waits for them, and re-layouts: 17.8 us -> 3.06 us
  Pallas kernels: 139 us -> 131 us
    unnamed x7 -> x2, local copies, waits for them, and re-layouts: 11.3 us -> 3.06 us
    pallas_call x1, Pallas kernels: 139 us -> 131 us  [on_device(): pl.pallas_call(kernel, name='sections', out_shape=(block, block), in_spec...]
    pallas_call x2 -> x0, local copies, waits for them, and re-layouts: 3.26 us -> none  [on_device(): pl.pallas_call(kernel, name='sections', out_shape=(block, block), in_spec...]
    another operation x2 -> x0, local copies, waits for them, and re-layouts: 2.05 us -> none
where the time goes in v2:
time: 135 us; the launch traced here: 134 us
  Pallas kernels  131 us (97%)
  local copies, waits for them, and re-layouts  3.06 us (2%)
    pallas_call x1, Pallas kernels, on_device(): pl.pallas_call(kernel, name='sections', out_shape=(block, block), in_spec...  131 us
    unnamed x2, local copies, waits for them, and re-layouts  3.06 us

profile of v2, /device:TPU:6, one launch (start us, length us, event | category | flops | bytes accessed | tf_op | source)
XLA Modules:
  0.0 134.4 jit_solution(3804786072145775472)
XLA Ops:
  0.6 130.7 %sections.1 = (bf16[336,128]{1,0:T(8,128)(2,1)}, bf16[336,128]{1,0:T(8,128)(2,1)}) custom-call(bf16[336,128]{1,0:T(8,128)(2,1)} %bitcast.23, f32[21,128]{1,0:T(8,128)} %bitcast.27, s32[6,1,128]{2,1,0:T(1,128)} %bitcast.28, f32[6,1,128]{2,1,0:T(1,128)} %bitcast.29, bf16[2,232,2688]{2,1,0:T(8,128)(2,1)} %bitcast.19, bf16[2,336,1856]{2,1,0:T(8,128)(2,1)} %bitcast.18, ...), custom_call_target="tpu_custom_call" | custom-call | tf_op jit(solution)/shard_map/sections/pallas_call | solution.py:567
  131.3 1.5 %copy.18 = bf16[1,128,336]{1,2,0:T(8,128)(2,1)} copy(bf16[1,128,336]{1,2,0:T(8,128)(2,1)} %bitcast.22) | data formatting | bytes 172032
  132.9 1.5 %copy.19 = bf16[1,128,336]{1,2,0:T(8,128)(2,1)} copy(bf16[1,128,336]{1,2,0:T(8,128)(2,1)} %bitcast.21) | data formatting | bytes 172032

commit v3 on v2

--- a/solution.py
+++ b/solution.py
@@ -263,7 +263,7 @@
     grads = []
 
     def attention_out(step):
-        if step == 0:
+        if step == 2:
             for load in loads[5:8]:
                 load.wait()
         to = lax.rem(x + step, NX)
@@ -306,7 +306,7 @@
     take(7)
     take(8)
     hop(5, 0)
-    attention_out(0)
+    attention_out(2)
     hop(5, 1)
     take(9)
     take(10)
@@ -318,8 +318,8 @@
     table = start(remote(tg, rtg, (tg_s, tg_r), 0, (other, yh, z, x, yl)))
     wait_all(*swap_up)
     share_up = start(remote(wuto.at[:, up_cols], wuto.at[:, up_cols], (w_s, w_r), 2, (other, yh, z, x, yl)))
-    attention_out(2)
     attention_out(3)
+    attention_out(0)
     unit = jnp.where(lanes == rows, 1.0, 0.0).astype(BF16)
 
     def turn_up(source, target):
@@ -477,44 +477,51 @@
     landed(back_b)
     combine(1)
 
-    def sum_right(k, half):
-        span = pl.ds(64 * half, 64)
+    def sum_right(k, piece):
+        span = pl.ds(32 * piece, 32)
         source = part.at[11 if k == 6 else 2 * k, span]
-        return remote(source, rs.at[k - 1, span], (rs_s, rs_r), 2 * (k - 1) + half, (s, yh, zr, x, yl))
-
-    def sum_left(k, half):
-        span = pl.ds(64 * half, 64)
+        return remote(source, rs.at[k - 1, span], (rs_s, rs_r), 4 * (k - 1) + piece, (s, yh, zr, x, yl))
+
+    def sum_left(k, piece):
+        span = pl.ds(32 * piece, 32)
         source = part.at[11 if k == 6 else 2 * k - 1, span]
-        return remote(source, rs.at[5 + k, span], (rs_s, rs_r), 2 * (5 + k) + half, (s, yh, zl, x, yl))
-
-    def add(slot, arrived, half):
-        span = slice(64 * half, 64 * half + 64)
+        return remote(source, rs.at[5 + k, span], (rs_s, rs_r), 4 * (5 + k) + piece, (s, yh, zl, x, yl))
+
+    def add(slot, arrived, piece):
+        span = slice(32 * piece, 32 * piece + 32)
         part[slot, span] = (part[slot, span].astype(F32) + rs[arrived, span].astype(F32)).astype(BF16)
 
-    forward = {0: start(sum_right(6, 0)), 1: start(sum_right(5, 1))}
-    backward = {1: start(sum_left(6, 1)), 0: start(sum_left(5, 0))}
+    forward, backward = {}, {}
+    for piece in range(2):
+        forward[piece] = start(sum_right(6, piece))
+        backward[piece + 2] = start(sum_left(6, piece + 2))
+    for piece in range(2):
+        forward[piece + 2] = start(sum_right(5, piece + 2))
+        backward[piece] = start(sum_left(5, piece))
 
     def write(out, total):
         for i in range(3):
             column_block = jnp.transpose(total[:, 128 * i : 128 * (i + 1)]).astype(BF16)
             out[128 * i : min(128 * (i + 1), FB), :] = column_block if i < 2 else column_block[0 : FB - 256]
 
+    for k in range(5, 0, -1):
+        for turn_of in range(4):
+            piece = turn_of
+            if k < 5 or piece < 2:
+                forward[piece].wait_recv()
+                add(2 * k, k, piece)
+                forward[piece] = start(sum_right(k, piece))
+            piece = turn_of ^ 2
+            if k < 5 or piece >= 2:
+                backward[piece].wait_recv()
+                add(2 * k - 1, 6 + k, piece)
+                backward[piece] = start(sum_left(k, piece))
     wait_all(*grads)
     total = gr[0].astype(F32)
     for i in range(1, 8):
         total = total + gr[i].astype(F32)
     write(grad_out, total)
-    for k in range(5, 0, -1):
-        for half in range(2):
-            if k < 5 or half == 0:
-                forward[half].wait_recv()
-                add(2 * k, k, half)
-                forward[half] = start(sum_right(k, half))
-            if k < 5 or half == 1:
-                backward[half].wait_recv()
-                add(2 * k - 1, 6 + k, half)
-                backward[half] = start(sum_left(k, half))
-    wait_all(forward[0], backward[0], forward[1], backward[1])
+    wait_all(*forward.values(), *backward.values())
     write(moe_out, part[0].astype(F32) + rs[0].astype(F32) + rs[6].astype(F32))
     for copy in sent:
         copy.wait_send()
@@ -560,7 +567,7 @@
         dma((8,)), dma((8,)),
         dma((8,)), dma((8,)),
         dma((16,)), dma((16,)),
-        dma((24,)), dma((24,)),
+        dma((48,)), dma((48,)),
         dma((8,)), dma((8,)),
     ]
     block = jax.ShapeDtypeStruct((FB, TOK), BF16)

time: 135 us -> 133 us (0.985)
  Pallas kernels: 131 us -> 129 us
    pallas_call x1, Pallas kernels: 131 us -> 129 us  [on_device(): pl.pallas_call(kernel, name='sections', out_shape=(block, block), in_spec...]
where the time goes in v3:
time: 133 us
  Pallas kernels  129 us (97%)
  local copies, waits for them, and re-layouts  3.06 us (2%)
    pallas_call x1, Pallas kernels, on_device(): pl.pallas_call(kernel, name='sections', out_shape=(block, block), in_spec...  129 us
    unnamed x2, local copies, waits for them, and re-layouts  3.06 us

profile of v3, /device:TPU:6, one launch (start us, length us, event | category | flops | bytes accessed | tf_op | source)
XLA Modules:
  0.0 132.8 jit_solution(15267886243883156768)
XLA Ops:
  0.6 129.1 %sections.1 = (bf16[336,128]{1,0:T(8,128)(2,1)}, bf16[336,128]{1,0:T(8,128)(2,1)}) custom-call(bf16[336,128]{1,0:T(8,128)(2,1)} %bitcast.23, f32[21,128]{1,0:T(8,128)} %bitcast.27, s32[6,1,128]{2,1,0:T(1,128)} %bitcast.28, f32[6,1,128]{2,1,0:T(1,128)} %bitcast.29, bf16[2,232,2688]{2,1,0:T(8,128)(2,1)} %bitcast.19, bf16[2,336,1856]{2,1,0:T(8,128)(2,1)} %bitcast.18, ...), custom_call_target="tpu_custom_call" | custom-call | tf_op jit(solution)/shard_map/sections/pallas_call | solution.py:574
  129.8 1.5 %copy.18 = bf16[1,128,336]{1,2,0:T(8,128)(2,1)} copy(bf16[1,128,336]{1,2,0:T(8,128)(2,1)} %bitcast.22) | data formatting | bytes 172032
  131.3 1.5 %copy.19 = bf16[1,128,336]{1,2,0:T(8,128)(2,1)} copy(bf16[1,128,336]{1,2,0:T(8,128)(2,1)} %bitcast.21) | data formatting | bytes 172032

commit v4 on v3

--- a/solution.py
+++ b/solution.py
@@ -283,6 +283,19 @@
         elif k == 5:
             hops[6, half] = (start(left(6, 1) if half else right(6, 0)),)
 
+    def spread(buf, sems, chunk):
+        a = start(remote(buf.at[x], buf.at[x], sems, chunk * 4, (s, yh, z, xr, yl)))
+        b = start(remote(buf.at[x], buf.at[x], sems, chunk * 4 + 1, (s, yh, z, xl, yl)))
+        return a, b
+
+    def relay(buf, sems, chunk, nearer, lower, upper):
+        nearer[0].wait_recv()
+        a = start(remote(buf.at[(xl, *lower)], buf.at[(xl, *lower)], sems, chunk * 4 + 2, (s, yh, z, xr, yl)))
+        nearer[1].wait_recv()
+        b = start(remote(buf.at[(xr, *upper)], buf.at[(xr, *upper)], sems, chunk * 4 + 3, (s, yh, z, xl, yl)))
+        return a, b
+
+    up_sems, hid_sems = (xg_s, xg_r), (hg_s, hg_r)
     take(0)
     attention_grad(0)
     hop(1, 0)
@@ -316,6 +329,8 @@
     take(11)
     arrive_b = dispatch(1)
     table = start(remote(tg, rtg, (tg_s, tg_r), 0, (other, yh, z, x, yl)))
+    wait_all(*arrive_a)
+    near_a = spread(xa, up_sems, 0)
     wait_all(*swap_up)
     share_up = start(remote(wuto.at[:, up_cols], wuto.at[:, up_cols], (w_s, w_r), 2, (other, yh, z, x, yl)))
     attention_out(3)
@@ -339,21 +354,6 @@
         lax.fori_loop(0, HID // 128, step, 0)
         target[1792:1856, :] = mm_nt(unit[0:64, 0:64], source[:, 1792:1856]).astype(BF16)
 
-    def spread(buf, sems, chunk):
-        a = start(remote(buf.at[x], buf.at[x], sems, chunk * 4, (s, yh, z, xr, yl)))
-        b = start(remote(buf.at[x], buf.at[x], sems, chunk * 4 + 1, (s, yh, z, xl, yl)))
-        return a, b
-
-    def relay(buf, sems, chunk, nearer, lower, upper):
-        nearer[0].wait_recv()
-        a = start(remote(buf.at[(xl, *lower)], buf.at[(xl, *lower)], sems, chunk * 4 + 2, (s, yh, z, xr, yl)))
-        nearer[1].wait_recv()
-        b = start(remote(buf.at[(xr, *upper)], buf.at[(xr, *upper)], sems, chunk * 4 + 3, (s, yh, z, xl, yl)))
-        return a, b
-
-    up_sems, hid_sems = (xg_s, xg_r), (hg_s, hg_r)
-    wait_all(*arrive_a)
-    near_a = spread(xa, up_sems, 0)
     loads[8].wait()
     turn_up(wut, wu)
     wait_all(*arrive_b)

time: 133 us -> 135 us (1.015)
  no operation moved by 1% of the time
where the time goes in v4:
time: 135 us; the launch traced here: 133 us
  Pallas kernels  130 us (96%)
  local copies, waits for them, and re-layouts  3.06 us (2%)
    pallas_call x1, Pallas kernels, on_device(): pl.pallas_call(kernel, name='sections', out_shape=(block, block), in_spec...  130 us
    unnamed x2, local copies, waits for them, and re-layouts  3.06 us

profile of v4, /device:TPU:6, one launch (start us, length us, event | category | flops | bytes accessed | tf_op | source)
XLA Modules:
  0.0 133.5 jit_solution(7046613730539998652)
XLA Ops:
  0.6 129.8 %sections.1 = (bf16[336,128]{1,0:T(8,128)(2,1)}, bf16[336,128]{1,0:T(8,128)(2,1)}) custom-call(bf16[336,128]{1,0:T(8,128)(2,1)} %bitcast.23, f32[21,128]{1,0:T(8,128)} %bitcast.27, s32[6,1,128]{2,1,0:T(1,128)} %bitcast.28, f32[6,1,128]{2,1,0:T(1,128)} %bitcast.29, bf16[2,232,2688]{2,1,0:T(8,128)(2,1)} %bitcast.19, bf16[2,336,1856]{2,1,0:T(8,128)(2,1)} %bitcast.18, ...), custom_call_target="tpu_custom_call" | custom-call | tf_op jit(solution)/shard_map/sections/pallas_call | solution.py:574
  130.4 1.5 %copy.18 = bf16[1,128,336]{1,2,0:T(8,128)(2,1)} copy(bf16[1,128,336]{1,2,0:T(8,128)(2,1)} %bitcast.22) | data formatting | bytes 172032
  132.0 1.5 %copy.19 = bf16[1,128,336]{1,2,0:T(8,128)(2,1)} copy(bf16[1,128,336]{1,2,0:T(8,128)(2,1)} %bitcast.21) | data formatting | bytes 172032
